TPU v7x, 32 devices: a whole 2x2x4 slice. The times are simulated.
32 devices in a mesh: members: 2 (over x), nodes: 16 (over z, y, core).
Axes of the slice: x: 2, y: 2, z: 4, core: 2. Of those that a mesh axis runs over, the one named last changes fastest.
Arguments:
- wave_state: float32 [16384, 1296], P(('members', 'nodes')), parts along dimension 0, may hold values from -6 to 6
- pool_weight: float32 [8192], P('nodes'), may hold values from -0.5 to 0.5
- lift_weight: float32 [8192], P('nodes'), may hold values from -8 to 8
- coarse_matrix: bfloat16 [64, 64], replicated, may hold values from -0.75 to 0.75
- block_matrix: float32 [16, 20, 128, 128], P('nodes'), may hold values from -0.25 to 0.25
- edge_dst: int32 [16, 20], P('nodes'), may hold values from 0 to 3
- edge_src: int32 [16, 20], P('nodes'), may hold values from 0 to 11
- edge_count: int32 [16], P('nodes'), may hold values from 10 to 20, as said below
- send_list: int32 [16, 4, 2], P('nodes'), may hold values from 0 to 3
- norm_gain: float32 [1296], replicated, may hold values from 0.1 to 1.9
- proj_in: bfloat16 [1296, 1024], replicated, may hold values from -0.15625 to 0.15625
- proj_out: bfloat16 [1024, 1296], replicated, may hold values from -0.1875 to 0.1875
Outputs:
- next_state: float32 [16384, 1296], P(('members', 'nodes')), parts along dimension 0
There are 2 independent parts, one for each index of `members`. A program takes and returns all parts, laid end to end along the dimension named above; an argument that names none is the same for every part. Nothing has to cross between parts.
Inputs may be any that keep to these rules, and one draw needn't show every extreme that they name: `edge_count`: some partition has all 20 slots live.
All inputs are finite; a program needn't handle non-finite values.
Results may differ from a plain program's by a relative error of at most 0.0028.
Values may be sent and summed in bfloat16 or wider, within the bound.
A program may use at most 128 MiB of HBM per device.

v0:
```python
import jax
import jax.numpy as jnp
from jax import lax
from jax.sharding import PartitionSpec as P

BLOCK = 128


def from_behind(shard, axis, by):
    size = lax.axis_size(axis)
    return lax.ppermute(shard, axis, [(i, (i + by) % size) for i in range(size)])


def shards(
    wave_state,
    pool_weight,
    lift_weight,
    coarse_matrix,
    block_matrix,
    edge_dst,
    edge_src,
    edge_count,
    send_list,
    norm_gain,
    proj_in,
    proj_out,
):
    bin_count = wave_state.shape[1]
    blocks_own = wave_state.reshape(-1, BLOCK, bin_count)
    owned_count = blocks_own.shape[0]
    pooled = jnp.einsum(
        "nib,ni->nb",
        blocks_own,
        pool_weight.reshape(owned_count, BLOCK),
        precision=lax.Precision.HIGHEST,
    )
    pooled = pooled.astype(jnp.bfloat16)
    position = lax.axis_index("nodes")
    my_rows = lax.dynamic_slice_in_dim(coarse_matrix, position * owned_count, owned_count, 0)
    coarse = jnp.dot(
        my_rows,
        lax.all_gather(pooled, "nodes", axis=0, tiled=True),
        preferred_element_type=jnp.float32,
    )
    chosen = send_list[0]
    arrived = [None, None, None, None]
    for column, offset in enumerate((1, -1, 2, -2)):
        arrived[column] = from_behind(jnp.take(blocks_own, chosen[column], axis=0), "nodes", offset)
    extended = jnp.concatenate([blocks_own] + arrived, 0)
    sources = jnp.take(extended, edge_src[0], axis=0)
    product = jnp.einsum("eij,ejb->eib", block_matrix[0], sources, precision=lax.Precision.HIGHEST)
    slot_count = edge_src.shape[1]
    live_mask = (jnp.arange(slot_count, dtype=jnp.int32) < edge_count[0]).astype(jnp.float32)
    selector = (edge_dst[0][None, :] == jnp.arange(owned_count, dtype=jnp.int32)[:, None]).astype(
        jnp.float32
    )
    selector = selector * live_mask[None, :]
    moved = jnp.einsum("ne,eib->nib", selector, product, precision=lax.Precision.HIGHEST)
    field = (
        blocks_own
        + moved
        + lift_weight.reshape(owned_count, BLOCK)[:, :, None] * coarse[:, None, :]
    )
    flat = field.reshape(-1, bin_count)
    mean_square = jnp.mean(flat * flat, axis=1, keepdims=True)
    normed = (flat * lax.rsqrt(mean_square + 1e-06) * norm_gain).astype(jnp.bfloat16)
    pre_act = jnp.dot(normed, proj_in, preferred_element_type=jnp.float32)
    hidden = jax.nn.gelu(pre_act).astype(jnp.bfloat16)
    return flat + jnp.dot(hidden, proj_out, preferred_element_type=jnp.float32)


def solution(mesh):
    in_specs = (
        P(("members", "nodes"), None),
        P("nodes"),
        P("nodes"),
        P(),
        P("nodes", None, None, None),
        P("nodes", None),
        P("nodes", None),
        P("nodes"),
        P("nodes", None, None),
        P(),
        P(),
        P(),
    )
    out_specs = P(("members", "nodes"), None)
    return jax.shard_map(shards, mesh=mesh, in_specs=in_specs, out_specs=out_specs, check_vma=False)
```

profile of v0, /device:TPU:0, one launch (start us, length us, event | category | flops | bytes accessed | tf_op | source)
XLA Modules:
  0.0 207.8 jit_solution(2417174646022189351)
XLA Ops:
  0.0 0.0 copy-start
  0.0 1.1 slice_reduce_fusion
  1.1 3.4 %copy_bitcast_fusion = f32[4,128,1296]{1,2,0:T(8,128)} fusion(f32[512,1296]{0,1:T(8,128)} %param.14), kind=kLoop, calls=%fused_computation.17 | loop fusion | bytes 5308416 | tf_op jit(solution)/shard_map/reshape | solution.py:29
  4.6 3.5 %gather_fusion.1 = f32[2,128,1296]{1,2,0:T(8,128)} fusion(f32[4,128,1296]{1,2,0:T(8,128)} %copy_bitcast_fusion, s32[1024]{0:T(1024)S(1)} %pad_clamp_fusion.4), kind=kCustom, calls=%fused_computation.clone | custom fusion | bytes 2654216 | tf_op jit(solution)/shard_map/jit(_take)/gather | solution.py:48
  8.0 5.8 %copy_select_fusion.3 = f32[2,128,1296]{1,0,2:T(2,128)} fusion(f32[2,128,1296]{1,2,0:T(8,128)} %gather_fusion.1, pred[2]{0:T(512)(128)(4,1)S(1)} %compare_and_fusion.3), kind=kLoop, calls=%fused_computation.32 | loop fusion | flops 331776 | bytes 2654210 | tf_op jit(solution)/shard_map/jit(_take)/select_n | solution.py:48
  13.8 0.5 collective-permute-start
  14.3 3.5 %gather_fusion.2 = f32[2,128,1296]{1,2,0:T(8,128)} fusion(f32[4,128,1296]{1,2,0:T(8,128)} %copy_bitcast_fusion, s32[1024]{0:T(1024)S(1)} %pad_clamp_fusion.3), kind=kCustom, calls=%fused_computation.1.clone | custom fusion | bytes 2654216 | tf_op jit(solution)/shard_map/jit(_take)/gather | solution.py:48
  17.7 5.7 %copy_select_fusion.2 = f32[2,128,1296]{1,0,2:T(2,128)} fusion(f32[2,128,1296]{1,2,0:T(8,128)} %gather_fusion.2, pred[2]{0:T(512)(128)(4,1)S(1)} %compare_and_fusion.2), kind=kLoop, calls=%fused_computation.31 | loop fusion | flops 331776 | bytes 2654210 | tf_op jit(solution)/shard_map/jit(_take)/select_n | solution.py:48
  23.5 5.0 %collective-permute-start.1 = (f32[2,128,1296]{1,0,2:T(2,128)}, f32[2,128,1296]{1,0,2:T(2,128)}, u32[]{:S(2)}, u32[]{:S(2)}) collective-permute-start(f32[2,128,1296]{1,0,2:T(2,128)} %copy_select_fusion.2), channel_id=1, source_target_pairs={{0,15},{1,0},{2,1},{3,2},{4,3},{5,4},{6,5},{7,6},{8,7},{9,8},{10,9... | collective-permute-start | bytes 3981320 | tf_op jit(solution)/shard_map/ppermute | solution.py:11
  28.5 3.5 %gather_fusion.3 = f32[2,128,1296]{1,2,0:T(8,128)} fusion(f32[4,128,1296]{1,2,0:T(8,128)} %copy_bitcast_fusion, s32[1024]{0:T(1024)S(1)} %pad_clamp_fusion.2), kind=kCustom, calls=%fused_computation.2.clone | custom fusion | bytes 2654216 | tf_op jit(solution)/shard_map/jit(_take)/gather | solution.py:48
  31.9 5.7 %copy_select_fusion.1 = f32[2,128,1296]{1,0,2:T(2,128)} fusion(f32[2,128,1296]{1,2,0:T(8,128)} %gather_fusion.3, pred[2]{0:T(512)(128)(4,1)S(1)} %compare_and_fusion.1), kind=kLoop, calls=%fused_computation.30 | loop fusion | flops 331776 | bytes 2654210 | tf_op jit(solution)/shard_map/jit(_take)/select_n | solution.py:48
  37.7 0.0 collective-permute-start.2
  37.7 3.5 %gather_fusion.4 = f32[2,128,1296]{1,2,0:T(8,128)} fusion(f32[4,128,1296]{1,2,0:T(8,128)} %copy_bitcast_fusion, s32[1024]{0:T(1024)S(1)} %pad_clamp_fusion.1), kind=kCustom, calls=%fused_computation.3.clone | custom fusion | bytes 2654216 | tf_op jit(solution)/shard_map/jit(_take)/gather | solution.py:48
  41.2 5.8 %copy_select_fusion = f32[2,128,1296]{1,0,2:T(2,128)} fusion(f32[2,128,1296]{1,2,0:T(8,128)} %gather_fusion.4, pred[2]{0:T(512)(128)(4,1)S(1)} %compare_and_fusion), kind=kLoop, calls=%fused_computation.29 | loop fusion | flops 331776 | bytes 2654210 | tf_op jit(solution)/shard_map/jit(_take)/select_n | solution.py:48
  46.9 0.0 copy-start.3
  46.9 4.7 %collective-permute-start.3 = (f32[2,128,1296]{1,0,2:T(2,128)}, f32[2,128,1296]{1,0,2:T(2,128)}, u32[]{:S(2)}, u32[]{:S(2)}) collective-permute-start(f32[2,128,1296]{1,0,2:T(2,128)} %copy_select_fusion), channel_id=1, source_target_pairs={{0,14},{1,15},{2,0},{3,1},{4,2},{5,3},{6,4},{7,5},{8,6},{9,7},{10,... | collective-permute-start | bytes 3981320 | tf_op jit(solution)/shard_map/ppermute | solution.py:11
  51.7 4.0 %reshape.81 = f32[4,128,1296]{1,0,2:T(4,128)} reshape(f32[512,1296]{0,1:T(8,128)} %param.14) | data formatting | bytes 5308416 | tf_op jit(solution)/shard_map/reshape | solution.py:29
  55.7 0.0 copy-start.6
  55.7 0.0 copy-done.3
  55.7 4.1 %fusion.46 = bf16[4,1,1296]{2,1,0:T(2,128)(2,1)S(1)} fusion(f32[4,128,1]{1,2,0:T(1,128)S(1)} %bitcast.68, f32[512,1296]{0,1:T(8,128)} %param.14), kind=kOutput, calls=%fused_computation.76 | convolution fusion | flops 7962624 | bytes 2666624 | tf_op jit(solution)/shard_map/nib,ni->nb/dot_general | solution.py:31
  59.8 57.5 %all-gather = bf16[16,4,1296]{2,1,0:T(4,128)(2,1)S(1)} all-gather(bf16[1,4,1296]{2,1,0:T(4,128)(2,1)S(1)} %bitcast.66), channel_id=1, replica_groups=mesh['members'=2,'nodes'=16] {'nodes'}, dimensions={0}, use_global_device_ids=true | all-gather | bytes 176256 | tf_op jit(solution)/shard_map/all_gather | solution.py:42
  117.3 0.1 reshape.129
  118.1 0.0 copy-done.6
  118.1 1.0 fusion.33
  119.1 0.0 collective-permute-done
  119.1 0.0 collective-permute-done.1
  119.1 0.0 collective-permute-done.2
  119.1 0.0 collective-permute-done.3
  119.1 26.5 %concatenate.3 = f32[12,128,1296]{1,0,2:T(8,128)} concatenate(f32[4,128,1296]{1,0,2:T(4,128)} %reshape.81, f32[2,128,1296]{1,0,2:T(2,128)} %collective-permute-done, f32[2,128,1296]{1,0,2:T(2,128)} %collective-permute-done.1, f32[2,128,1296]{1,0,2:T(2,128)} %collective-permute-done.2, f32[2,128,1296]{1,0,2:T(2,128)} %collective-permute-done.3), dimensions={0} | concatenate | bytes 15925248 | tf_op jit(solution)/shard_map/concatenate | solution.py:49
  145.6 9.6 %copy.32 = f32[12,128,1296]{1,2,0:T(8,128)} copy(f32[12,128,1296]{1,0,2:T(8,128)} %concatenate.3) | data formatting | bytes 15925248 | tf_op jit(solution)/shard_map/concatenate | solution.py:49
  155.3 11.0 %gather_fusion = f32[20,128,1296]{1,2,0:T(8,128)} fusion(f32[12,128,1296]{1,2,0:T(8,128)} %copy.32, s32[1024]{0:T(1024)S(1)} %pad_clamp_fusion), kind=kCustom, calls=%fused_computation.4 | custom fusion | bytes 26542160 | tf_op jit(solution)/shard_map/jit(_take)/gather | solution.py:50
  166.3 0.0 copy-start.1
  166.3 0.0 copy-start.2
  166.3 0.0 copy-start.4
  166.3 15.0 %fusion.4 = f32[20,128,1296]{1,2,0:T(8,128)S(1)} fusion(f32[20,128,1296]{1,2,0:T(8,128)} %gather_fusion, pred[20]{0:T(512)(128)(4,1)S(1)} %compare_and_fusion.4, f32[1,20,128,128]{3,2,1,0:T(8,128)} %param.18), kind=kOutput, calls=%fused_computation.9 | convolution fusion | flops 5099397120 | bytes 27852820 | tf_op jit(solution)/shard_map/eij,ejb->eib/dot_general | solution.py:51
  181.3 0.0 copy-done.1
  181.3 0.0 copy-done.2
  181.4 0.0 copy-done.4
  181.4 0.0 copy-start.5
  181.4 18.1 %multiply_reduce_fusion = (f32[4,128]{1,0:T(4,128)S(1)}, f32[4,128,1296]{1,0,2:T(4,128)}) fusion(f32[4,1296]{0,1:T(8,128)S(1)} %fusion.33, f32[4,128]{1,0:T(4,128)S(1)} %bitcast.67, f32[4,128,1296]{1,0,2:T(4,128)S(1)} %copy-done.1, f32[20,128,1296]{1,2,0:T(8,128)S(1)} %fusion.4, f32[20]{0:T(128)S(1)} %compare_convert_fusion, s32[20]{0:T(128)S(1)} %bitcast.69), kind=kOutput, calls=%fused_computation.18 | convolution fusion | flops 162569888 | bytes 18604448 | tf_op jit(solution)/shard_map/ne,eib->nib/dot_general | solution.py:58
  199.5 0.0 copy-done
  199.5 0.0 copy-done.5
  199.5 8.4 %convolution_add_fusion = f32[512,1296]{0,1:T(8,128)} fusion(bf16[1024,1296]{0,1:T(8,128)(2,1)S(1)} %copy-done, f32[162,8,4,128]{3,2,1,0:T(4,128)} %bitcast.65, bf16[1296,1024]{1,0:T(8,128)(2,1)} %param.24, f32[1296]{0:T(1024)S(1)} %copy-done.5, f32[512]{0:T(512)S(1)} %rsqrt_bitcast_fusion), kind=kOutput, calls=%fused_computation.12 | convolution fusion | flops 2725281792 | bytes 10624064 | tf_op jit(solution)/shard_map/dot_general | solution.py:69
  (18 shorter events, 0.1 us)
Async XLA Ops:
  0.0 199.5 %copy-start = (bf16[1024,1296]{0,1:T(8,128)(2,1)S(1)}, bf16[1024,1296]{0,1:T(8,128)(2,1)}, u32[]{:S(2)}) copy-start(bf16[1024,1296]{0,1:T(8,128)(2,1)} %param.25) | copy-start | bytes 7962628
  13.8 105.3 %collective-permute-start = (f32[2,128,1296]{1,0,2:T(2,128)}, f32[2,128,1296]{1,0,2:T(2,128)}, u32[]{:S(2)}, u32[]{:S(2)}) collective-permute-start(f32[2,128,1296]{1,0,2:T(2,128)} %copy_select_fusion.3), channel_id=1, source_target_pairs={{0,1},{1,2},{2,3},{3,4},{4,5},{5,6},{6,7},{7,8},{8,9},{9,10},{10,1... | collective-permute-start | bytes 3981320 | tf_op jit(solution)/shard_map/ppermute | solution.py:11
  23.5 95.7 %collective-permute-start.1 = (f32[2,128,1296]{1,0,2:T(2,128)}, f32[2,128,1296]{1,0,2:T(2,128)}, u32[]{:S(2)}, u32[]{:S(2)}) collective-permute-start(f32[2,128,1296]{1,0,2:T(2,128)} %copy_select_fusion.2), channel_id=1, source_target_pairs={{0,15},{1,0},{2,1},{3,2},{4,3},{5,4},{6,5},{7,6},{8,7},{9,8},{10,9... | collective-permute-start | bytes 3981320 | tf_op jit(solution)/shard_map/ppermute | solution.py:11
  37.7 81.5 %collective-permute-start.2 = (f32[2,128,1296]{1,0,2:T(2,128)}, f32[2,128,1296]{1,0,2:T(2,128)}, u32[]{:S(2)}, u32[]{:S(2)}) collective-permute-start(f32[2,128,1296]{1,0,2:T(2,128)} %copy_select_fusion.1), channel_id=1, source_target_pairs={{0,2},{1,3},{2,4},{3,5},{4,6},{5,7},{6,8},{7,9},{8,10},{9,11},{10,... | collective-permute-start | bytes 3981320 | tf_op jit(solution)/shard_map/ppermute | solution.py:11
  46.9 8.8 %copy-start.3 = (f32[512]{0:T(512)S(1)}, f32[512]{0:T(512)}, u32[]{:S(2)}) copy-start(f32[512]{0:T(512)} %param.15) | copy-start | bytes 6148
  46.9 72.2 %collective-permute-start.3 = (f32[2,128,1296]{1,0,2:T(2,128)}, f32[2,128,1296]{1,0,2:T(2,128)}, u32[]{:S(2)}, u32[]{:S(2)}) collective-permute-start(f32[2,128,1296]{1,0,2:T(2,128)} %copy_select_fusion), channel_id=1, source_target_pairs={{0,14},{1,15},{2,0},{3,1},{4,2},{5,3},{6,4},{7,5},{8,6},{9,7},{10,... | collective-permute-start | bytes 3981320 | tf_op jit(solution)/shard_map/ppermute | solution.py:11
  55.7 62.4 %copy-start.6 = (s32[1,20]{1,0:T(1,128)S(1)}, s32[1,20]{1,0:T(1,128)}, u32[]{:S(2)}) copy-start(s32[1,20]{1,0:T(1,128)} %param.20) | copy-start | bytes 244
  166.3 15.0 %copy-start.1 = (f32[4,128,1296]{1,0,2:T(4,128)S(1)}, f32[4,128,1296]{1,0,2:T(4,128)}, u32[]{:S(2)}) copy-start(f32[4,128,1296]{1,0,2:T(4,128)} %reshape.81) | copy-start | bytes 7962628
  166.3 15.0 %copy-start.2 = (f32[512]{0:T(512)S(1)}, f32[512]{0:T(512)}, u32[]{:S(2)}) copy-start(f32[512]{0:T(512)} %param.16) | copy-start | bytes 6148
  166.3 15.0 %copy-start.4 = (s32[1,20]{1,0:T(1,128)S(1)}, s32[1,20]{1,0:T(1,128)}, u32[]{:S(2)}) copy-start(s32[1,20]{1,0:T(1,128)} %param.19) | copy-start | bytes 244
  181.4 18.1 %copy-start.5 = (f32[1296]{0:T(1024)S(1)}, f32[1296]{0:T(1024)}, u32[]{:S(2)}) copy-start(f32[1296]{0:T(1024)} %param.23) | copy-start | bytes 15556
where the time goes:
time: 210 us; the launch traced here: 208 us
  local copies, waits for them, and re-layouts  69.7 us (33%)
  blocking collectives  57.5 us (27%)
  matrix products  46.5 us (22%)
  other arithmetic  23.1 us (11%)
  starting transfers between devices  10.2 us (5%)
    all_gather x1, blocking collectives, shards(): lax.all_gather(pooled, 'nodes', axis=0, tiled=True)  57.5 us
    concatenate x2, local copies, waits for them, and re-layouts, shards(): extended = jnp.concatenate([blocks_own] + arrived, 0)  36.1 us
    select_n x8, other arithmetic, shards(): jnp.take(blocks_own, chosen[column], axis=0)  23 us
    dot_general x1, matrix products, shards(): jnp.einsum('ne,eib->nib', selector, product, precision=lax.Precision.HIGH...  18.1 us
    dot_general x1, matrix products, shards(): jnp.einsum('eij,ejb->eib', block_matrix[0], sources, precision=lax.Precis...  15 us
    gather x4, local copies, waits for them, and re-layouts, shards(): jnp.take(blocks_own, chosen[column], axis=0)  13.9 us
    gather x1, local copies, waits for them, and re-layouts, shards(): sources = jnp.take(extended, edge_src[0], axis=0)  11 us
    ppermute x4, starting transfers between devices, from_behind(): lax.ppermute(shard, axis, [(i, (i + by) % size) for i in range(size)])  10.2 us
  transfers between devices with their start and end apart: 4, of which 0 were waited for; matrix products, arithmetic and copies ran while one was open for 18% of the time, Pallas kernels for 0%

commit v1 on v0

--- a/solution.py
+++ b/solution.py
@@ -43,19 +43,20 @@
         preferred_element_type=jnp.float32,
     )
     chosen = send_list[0]
+    narrow = blocks_own.astype(jnp.bfloat16)
     arrived = [None, None, None, None]
     for column, offset in enumerate((1, -1, 2, -2)):
-        arrived[column] = from_behind(jnp.take(blocks_own, chosen[column], axis=0), "nodes", offset)
-    extended = jnp.concatenate([blocks_own] + arrived, 0)
+        arrived[column] = from_behind(jnp.take(narrow, chosen[column], axis=0), "nodes", offset)
+    extended = jnp.concatenate([narrow] + arrived, 0)
     sources = jnp.take(extended, edge_src[0], axis=0)
-    product = jnp.einsum("eij,ejb->eib", block_matrix[0], sources, precision=lax.Precision.HIGHEST)
     slot_count = edge_src.shape[1]
-    live_mask = (jnp.arange(slot_count, dtype=jnp.int32) < edge_count[0]).astype(jnp.float32)
-    selector = (edge_dst[0][None, :] == jnp.arange(owned_count, dtype=jnp.int32)[:, None]).astype(
-        jnp.float32
-    )
-    selector = selector * live_mask[None, :]
-    moved = jnp.einsum("ne,eib->nib", selector, product, precision=lax.Precision.HIGHEST)
+    live_mask = jnp.arange(slot_count, dtype=jnp.int32) < edge_count[0]
+    selector = (edge_dst[0][None, :] == jnp.arange(owned_count, dtype=jnp.int32)[:, None]) & live_mask[None, :]
+    weights = block_matrix[0].transpose(1, 0, 2).reshape(BLOCK, -1).astype(jnp.bfloat16)
+    spread = jnp.repeat(selector, BLOCK, axis=1)
+    weights = jnp.where(spread[:, None, :], weights[None], 0).reshape(owned_count * BLOCK, -1)
+    moved = jnp.dot(weights, sources.reshape(-1, bin_count), preferred_element_type=jnp.float32)
+    moved = moved.reshape(owned_count, BLOCK, bin_count)
     field = (
         blocks_own
         + moved

time: 210 us -> 117 us (0.56)
  local copies, waits for them, and re-layouts: 69.7 us -> 39.3 us
  matrix products: 46.5 us -> 17.9 us
  blocking collectives: 57.5 us -> 40.2 us
  other arithmetic: 23.1 us -> 8.06 us
    concatenate x2 -> x1, local copies, waits for them, and re-layouts: 36.1 us -> 1.97 us  [shards(): extended = jnp.concatenate([narrow] + arrived, 0)]
    dot_general x2 -> x1, matrix products: 33.1 us -> 5.61 us  [shards(): jnp.dot(weights, sources.reshape(-1, bin_count), preferred_element_type=j...]
    select_n x8, other arithmetic: 23 us -> 3.98 us  [shards(): jnp.take(narrow, chosen[column], axis=0)]
    all_gather x1, blocking collectives: 57.5 us -> 40.2 us  [shards(): lax.all_gather(pooled, 'nodes', axis=0, tiled=True)]
    unnamed x15 -> x22, local copies, waits for them, and re-layouts: 0.11 us -> 10.3 us
    reshape x2 -> x0, local copies, waits for them, and re-layouts: 7.45 us -> none  [shards(): blocks_own = wave_state.reshape(-1, BLOCK, bin_count)]
    gather x4, local copies, waits for them, and re-layouts: 13.9 us -> 7.99 us  [shards(): jnp.take(narrow, chosen[column], axis=0)]
    gather x1 -> x2, local copies, waits for them, and re-layouts: 11 us -> 16.7 us  [shards(): sources = jnp.take(extended, edge_src[0], axis=0)]
where the time goes in v1:
time: 117 us; the launch traced here: 116 us
  blocking collectives  40.2 us (34%)
  local copies, waits for them, and re-layouts  39.3 us (34%)
  matrix products  17.9 us (15%)
  starting transfers between devices  10.2 us (9%)
  other arithmetic  8.06 us (7%)
    all_gather x1, blocking collectives, shards(): lax.all_gather(pooled, 'nodes', axis=0, tiled=True)  40.2 us
    gather x2, local copies, waits for them, and re-layouts, shards(): sources = jnp.take(extended, edge_src[0], axis=0)  16.7 us
    unnamed x22, local copies, waits for them, and re-layouts  10.3 us
    ppermute x4, starting transfers between devices, from_behind(): lax.ppermute(shard, axis, [(i, (i + by) % size) for i in range(size)])  10.2 us
    dot_general x1, matrix products, shards(): return flat + jnp.dot(hidden, proj_out, preferred_element_type=jnp.float32)  9.12 us
    gather x4, local copies, waits for them, and re-layouts, shards(): jnp.take(narrow, chosen[column], axis=0)  7.99 us
    dot_general x1, matrix products, shards(): jnp.dot(weights, sources.reshape(-1, bin_count), preferred_element_type=j...  5.61 us
    select_n x2, other arithmetic, shards(): sources = jnp.take(extended, edge_src[0], axis=0)  4 us
  transfers between devices with their start and end apart: 4, of which 0 were waited for; matrix products, arithmetic and copies ran while one was open for 18% of the time, Pallas kernels for 0%

profile of v1, /device:TPU:0, one launch (start us, length us, event | category | flops | bytes accessed | tf_op | source)
XLA Modules:
  0.0 116.4 jit_solution(9931511660682392945)
XLA Ops:
  0.0 0.0 copy-start
  0.0 1.1 slice_reduce_fusion
  1.1 0.7 copy-done
  1.8 1.8 %constant_dynamic-update-slice_fusion.4 = (bf16[12,128,1296]{1,2,0:T(8,128)(2,1)}, bf16[4,128,1296]{1,2,0:T(8,128)(2,1)}) fusion(f32[512,1296]{0,1:T(8,128)S(1)} %copy-done), kind=kLoop, calls=%fused_computation.47 | loop fusion | bytes 5308416
  3.7 2.0 %gather_fusion.1 = bf16[2,128,1296]{1,2,0:T(8,128)(2,1)S(1)} fusion(bf16[4,128,1296]{1,2,0:T(8,128)(2,1)} %get-tuple-element.11, s32[1024]{0:T(1024)S(1)} %get-tuple-element.17), kind=kCustom, calls=%fused_computation.clone | custom fusion | bytes 1327112 | tf_op jit(solution)/shard_map/jit(_take)/gather | solution.py:49
  5.7 1.0 broadcast_select_fusion.3
  6.7 0.5 collective-permute-start
  7.2 2.0 %gather_fusion.2 = bf16[2,128,1296]{1,2,0:T(8,128)(2,1)S(1)} fusion(bf16[4,128,1296]{1,2,0:T(8,128)(2,1)} %get-tuple-element.11, s32[1024]{0:T(1024)S(1)} %get-tuple-element.16), kind=kCustom, calls=%fused_computation.1.clone | custom fusion | bytes 1327112 | tf_op jit(solution)/shard_map/jit(_take)/gather | solution.py:49
  9.2 1.0 broadcast_select_fusion.2
  10.1 5.0 %collective-permute-start.1 = (bf16[2,128,1296]{1,2,0:T(8,128)(2,1)}, bf16[2,128,1296]{1,2,0:T(8,128)(2,1)}, u32[]{:S(2)}, u32[]{:S(2)}) collective-permute-start(bf16[2,128,1296]{1,2,0:T(8,128)(2,1)} %broadcast_select_fusion.2), channel_id=1, source_target_pairs={{0,15},{1,0},{2,1},{3,2},{4,3},{5,4},{6,5},{7,6},{8,7},{9,8},{10,9... | collective-permute-start | bytes 1990664 | tf_op jit(solution)/shard_map/ppermute | solution.py:11
  15.2 0.0 copy-start.2
  15.2 2.0 %gather_fusion.3 = bf16[2,128,1296]{1,2,0:T(8,128)(2,1)S(1)} fusion(bf16[4,128,1296]{1,2,0:T(8,128)(2,1)} %get-tuple-element.11, s32[1024]{0:T(1024)S(1)} %get-tuple-element.15), kind=kCustom, calls=%fused_computation.2.clone | custom fusion | bytes 1327112 | tf_op jit(solution)/shard_map/jit(_take)/gather | solution.py:49
  17.2 1.0 broadcast_select_fusion.1
  18.2 0.0 collective-permute-start.2
  18.2 2.0 %gather_fusion.4 = bf16[2,128,1296]{1,2,0:T(8,128)(2,1)S(1)} fusion(bf16[4,128,1296]{1,2,0:T(8,128)(2,1)} %get-tuple-element.11, s32[1024]{0:T(1024)S(1)} %get-tuple-element.14), kind=kCustom, calls=%fused_computation.3.clone | custom fusion | bytes 1327112 | tf_op jit(solution)/shard_map/jit(_take)/gather | solution.py:49
  20.2 0.0 copy-start.5
  20.2 0.0 copy-start.6
  20.2 1.0 broadcast_select_fusion
  21.2 4.7 %collective-permute-start.3 = (bf16[2,128,1296]{1,2,0:T(8,128)(2,1)}, bf16[2,128,1296]{1,2,0:T(8,128)(2,1)}, u32[]{:S(2)}, u32[]{:S(2)}) collective-permute-start(bf16[2,128,1296]{1,2,0:T(8,128)(2,1)} %broadcast_select_fusion), channel_id=1, source_target_pairs={{0,14},{1,15},{2,0},{3,1},{4,2},{5,3},{6,4},{7,5},{8,6},{9,7},{10,... | collective-permute-start | bytes 1990664 | tf_op jit(solution)/shard_map/ppermute | solution.py:11
  25.9 0.0 copy-done.2
  25.9 2.4 %fusion.10 = bf16[4,1,1296]{2,1,0:T(2,128)(2,1)S(1)} fusion(f32[4,128,1]{1,2,0:T(1,128)S(1)} %bitcast.87, f32[512,1296]{0,1:T(8,128)S(1)} %copy-done), kind=kOutput, calls=%fused_computation.15 | convolution fusion | flops 7962624 | bytes 2666624 | tf_op jit(solution)/shard_map/nib,ni->nb/dot_general | solution.py:31
  28.3 40.2 %all-gather = bf16[16,4,1296]{2,1,0:T(4,128)(2,1)S(1)} all-gather(bf16[1,4,1296]{2,1,0:T(4,128)(2,1)S(1)} %bitcast.85), channel_id=1, replica_groups=mesh['members'=2,'nodes'=16] {'nodes'}, dimensions={0}, use_global_device_ids=true | all-gather | bytes 176256 | tf_op jit(solution)/shard_map/all_gather | solution.py:42
  68.5 0.1 reshape.145
  69.2 0.0 copy-done.5
  69.2 0.1 broadcast_bitcast_fusion
  69.3 0.8 fusion.35
  70.1 0.0 copy-done.6
  70.2 0.1 broadcast_bitcast_fusion.1
  70.2 1.6 %copy.26 = bf16[1,20,128,128]{2,3,1,0:T(8,128)(2,1)S(1)} copy(f32[1,20,128,128]{3,2,1,0:T(8,128)} %param.18) | data formatting | bytes 1966080 | tf_op args[4]
  71.9 1.1 copy.27
  73.0 0.0 collective-permute-done
  73.0 2.0 %constant_dynamic-update-slice_fusion.3 = bf16[12,128,1296]{1,2,0:T(8,128)(2,1)} fusion(bf16[12,128,1296]{1,2,0:T(8,128)(2,1)} %get-tuple-element.10, bf16[2,128,1296]{1,2,0:T(8,128)(2,1)} %collective-permute-done), kind=kLoop, calls=%fused_computation.46 | loop fusion | bytes 1327104
  75.0 0.0 collective-permute-done.1
  75.0 2.0 %constant_dynamic-update-slice_fusion.2 = bf16[12,128,1296]{1,2,0:T(8,128)(2,1)} fusion(bf16[12,128,1296]{1,2,0:T(8,128)(2,1)} %constant_dynamic-update-slice_fusion.3, bf16[2,128,1296]{1,2,0:T(8,128)(2,1)} %collective-permute-done.1), kind=kLoop, calls=%fused_computation.45 | loop fusion | bytes 1327104
  77.0 0.0 collective-permute-done.2
  77.0 2.0 %constant_dynamic-update-slice_fusion.1 = bf16[12,128,1296]{1,2,0:T(8,128)(2,1)} fusion(bf16[12,128,1296]{1,2,0:T(8,128)(2,1)} %constant_dynamic-update-slice_fusion.2, bf16[2,128,1296]{1,2,0:T(8,128)(2,1)} %collective-permute-done.2), kind=kLoop, calls=%fused_computation.44 | loop fusion | bytes 1327104
  79.0 0.0 collective-permute-done.3
  79.0 2.0 %constant_dynamic-update-slice_fusion = bf16[12,128,1296]{1,2,0:T(8,128)(2,1)} fusion(bf16[12,128,1296]{1,2,0:T(8,128)(2,1)} %constant_dynamic-update-slice_fusion.1, bf16[2,128,1296]{1,2,0:T(8,128)(2,1)} %collective-permute-done.3), kind=kLoop, calls=%fused_computation.43 | loop fusion | bytes 1327104 | tf_op jit(solution)/shard_map/concatenate | solution.py:50
  81.0 7.0 %gather_fusion = bf16[20,128,1296]{1,2,0:T(8,128)(2,1)} fusion(bf16[12,128,1296]{1,2,0:T(8,128)(2,1)} %constant_dynamic-update-slice_fusion, s32[1024]{0:T(1024)S(1)} %pad_clamp_fusion), kind=kCustom, calls=%fused_computation.4 | custom fusion | bytes 13271120 | tf_op jit(solution)/shard_map/jit(_take)/gather | solution.py:51
  87.9 9.7 %copy.29 = bf16[20,128,1296]{2,1,0:T(8,128)(2,1)} copy(bf16[20,128,1296]{1,2,0:T(8,128)(2,1)} %gather_fusion) | data formatting | bytes 13271040 | tf_op jit(solution)/shard_map/jit(_take)/gather | solution.py:51
  97.7 0.0 copy-start.1
  97.7 4.0 %bitcast_select_fusion = bf16[2560,1296]{1,0:T(8,128)(2,1)S(1)} fusion(bf16[20,128,1296]{2,1,0:T(8,128)(2,1)} %copy.29, pred[2560]{0:T(1024)(128)(4,1)S(1)} %broadcast_bitcast_fusion.1), kind=kLoop, calls=%fused_computation.7 | loop fusion | flops 3317760 | bytes 13273600 | tf_op jit(solution)/shard_map/jit(_take)/select_n | solution.py:51
  101.7 0.0 copy-done.1
  101.7 0.0 copy-done.4
  101.7 0.0 copy-start.3
  101.7 5.6 %multiply_reduce_fusion = (f32[4,128]{1,0:T(4,128)S(1)}, f32[4,128,1296]{1,2,0:T(8,128)}) fusion(f32[4,1296]{1,0:T(4,128)S(1)} %fusion.35, f32[4,128]{1,0:T(4,128)S(1)} %bitcast.88, bf16[2560,1296]{1,0:T(8,128)(2,1)S(1)} %bitcast_select_fusion, pred[4,2560]{1,0:T(4,128)(4,1)S(1)} %bitcast.86, bf16[128,2560]{1,0:T(8,128)(2,1)S(1)} %copy-done.1, ...), kind=kOutput, calls=%fused_computation.18 | convolution fusion | flops 3402014208 | bytes 12634368 | tf_op jit(solution)/shard_map/dot_general | solution.py:58
  107.3 0.0 copy-done.3
  107.3 9.1 %convolution_add_fusion = f32[512,1296]{0,1:T(8,128)} fusion(bf16[1024,1296]{0,1:T(8,128)(2,1)} %param.25, bf16[1296,1024]{1,0:T(8,128)(2,1)} %param.24, f32[1296]{0:T(1024)S(1)} %copy-done.3, f32[512]{0:T(512)S(1)} %rsqrt_bitcast_fusion, f32[4,128,1296]{1,2,0:T(8,128)} %get-tuple-element.13), kind=kOutput, calls=%fused_computation.9 | convolution fusion | flops 2725281792 | bytes 10624064 | tf_op jit(solution)/shard_map/dot_general | solution.py:70
  (19 shorter events, 0.1 us)
Async XLA Ops:
  0.0 1.8 %copy-start = (f32[512,1296]{0,1:T(8,128)S(1)}, f32[512,1296]{0,1:T(8,128)}, u32[]{:S(2)}) copy-start(f32[512,1296]{0,1:T(8,128)} %param.14) | copy-start | bytes 7962628
  6.7 66.3 %collective-permute-start = (bf16[2,128,1296]{1,2,0:T(8,128)(2,1)}, bf16[2,128,1296]{1,2,0:T(8,128)(2,1)}, u32[]{:S(2)}, u32[]{:S(2)}) collective-permute-start(bf16[2,128,1296]{1,2,0:T(8,128)(2,1)} %broadcast_select_fusion.3), channel_id=1, source_target_pairs={{0,1},{1,2},{2,3},{3,4},{4,5},{5,6},{6,7},{7,8},{8,9},{9,10},{10,1... | collective-permute-start | bytes 1990664 | tf_op jit(solution)/shard_map/ppermute | solution.py:11
  10.1 64.9 %collective-permute-start.1 = (bf16[2,128,1296]{1,2,0:T(8,128)(2,1)}, bf16[2,128,1296]{1,2,0:T(8,128)(2,1)}, u32[]{:S(2)}, u32[]{:S(2)}) collective-permute-start(bf16[2,128,1296]{1,2,0:T(8,128)(2,1)} %broadcast_select_fusion.2), channel_id=1, source_target_pairs={{0,15},{1,0},{2,1},{3,2},{4,3},{5,4},{6,5},{7,6},{8,7},{9,8},{10,9... | collective-permute-start | bytes 1990664 | tf_op jit(solution)/shard_map/ppermute | solution.py:11
  15.2 10.8 %copy-start.2 = (f32[512]{0:T(512)S(1)}, f32[512]{0:T(512)}, u32[]{:S(2)}) copy-start(f32[512]{0:T(512)} %param.15) | copy-start | bytes 6148
  18.2 58.8 %collective-permute-start.2 = (bf16[2,128,1296]{1,2,0:T(8,128)(2,1)}, bf16[2,128,1296]{1,2,0:T(8,128)(2,1)}, u32[]{:S(2)}, u32[]{:S(2)}) collective-permute-start(bf16[2,128,1296]{1,2,0:T(8,128)(2,1)} %broadcast_select_fusion.1), channel_id=1, source_target_pairs={{0,2},{1,3},{2,4},{3,5},{4,6},{5,7},{6,8},{7,9},{8,10},{9,11},{10,... | collective-permute-start | bytes 1990664 | tf_op jit(solution)/shard_map/ppermute | solution.py:11
  20.2 49.0 %copy-start.5 = (s32[1,20]{1,0:T(1,128)S(1)}, s32[1,20]{1,0:T(1,128)}, u32[]{:S(2)}) copy-start(s32[1,20]{1,0:T(1,128)} %param.19) | copy-start | bytes 244
  20.2 49.9 %copy-start.6 = (s32[1,20]{1,0:T(1,128)S(1)}, s32[1,20]{1,0:T(1,128)}, u32[]{:S(2)}) copy-start(s32[1,20]{1,0:T(1,128)} %param.20) | copy-start | bytes 244
  21.2 57.8 %collective-permute-start.3 = (bf16[2,128,1296]{1,2,0:T(8,128)(2,1)}, bf16[2,128,1296]{1,2,0:T(8,128)(2,1)}, u32[]{:S(2)}, u32[]{:S(2)}) collective-permute-start(bf16[2,128,1296]{1,2,0:T(8,128)(2,1)} %broadcast_select_fusion), channel_id=1, source_target_pairs={{0,14},{1,15},{2,0},{3,1},{4,2},{5,3},{6,4},{7,5},{8,6},{9,7},{10,... | collective-permute-start | bytes 1990664 | tf_op jit(solution)/shard_map/ppermute | solution.py:11
  97.7 4.0 %copy-start.1 = (bf16[128,2560]{1,0:T(8,128)(2,1)S(1)}, bf16[128,2560]{1,0:T(8,128)(2,1)}, u32[]{:S(2)}) copy-start(bf16[128,2560]{1,0:T(8,128)(2,1)} %copy.27) | copy-start | bytes 1966084
  97.7 4.0 %copy-start.4 = (f32[512]{0:T(512)S(1)}, f32[512]{0:T(512)}, u32[]{:S(2)}) copy-start(f32[512]{0:T(512)} %param.16) | copy-start | bytes 6148
  101.7 5.6 %copy-start.3 = (f32[1296]{0:T(1024)S(1)}, f32[1296]{0:T(1024)}, u32[]{:S(2)}) copy-start(f32[1296]{0:T(1024)} %param.23) | copy-start | bytes 15556

commit v2 on v0

v2 whole, which is shorter than its diff:
```python
import functools

import jax
import jax.numpy as jnp
from jax import lax
from jax.experimental import pallas as pl
from jax.experimental.pallas import tpu as pltpu
from jax.sharding import PartitionSpec as P

BLOCK = 128
PIECE = 384
MESH = pl.DeviceIdType.MESH


def pieces_of(bins):
    out, start = [], 0
    while start < bins:
        width = min(PIECE, bins - start)
        out.append((start, width, -(-width // 128) * 128))
        start += width
    return out


def exchange_kernel(
    size, owned, pieces,
    state, columns, mixing, matrix, edge_dst, edge_src, edge_count, list_ref,
    field,
    weights, gathered, pooled, lists, lists_scalar, coarse,
    own_send, own_recv, list_send, list_recv, pool_send, pool_recv, local_sem,
    *ext,
):
    slots = matrix.shape[0]
    count = len(pieces)
    me = lax.axis_index("nodes")
    core = lax.rem(me, 2)
    chip = me // 2
    odd = lax.rem(chip, 2)
    mate = chip * 2 + 1 - core
    partner = (chip + 1 - 2 * odd) * 2 + core
    onward = lax.rem(me + 4 - 8 * odd + size, size)

    barrier = pltpu.get_barrier_semaphore()

    def greet(step, carry):
        pl.semaphore_signal(
            barrier, inc=1, device_id={"nodes": lax.rem(me + step, size)}, device_id_type=MESH
        )
        return carry

    lax.fori_loop(1, size, greet, 0)

    rows = []
    for number, (start, width, wide) in enumerate(pieces):
        for block in range(owned):
            part = state[block * BLOCK : (block + 1) * BLOCK, start : start + width]
            weight = columns[block * BLOCK : (block + 1) * BLOCK, 0:1]
            row = jnp.sum(part * weight, axis=0, keepdims=True)
            if width < wide:
                part = jnp.concatenate([part, jnp.zeros((BLOCK, wide - width), jnp.float32)], 1)
            if width < PIECE:
                row = jnp.concatenate([row, jnp.zeros((1, PIECE - width), jnp.float32)], 1)
            ext[number][block] = part.astype(jnp.bfloat16)
            rows.append(row)
    pooled[me] = jnp.concatenate(rows, 0).astype(jnp.bfloat16)

    pl.semaphore_wait(barrier, size - 1)

    def block_copy(number, kind, source, target):
        return pltpu.make_async_remote_copy(
            src_ref=ext[number].at[pl.ds(source * owned, owned)],
            dst_ref=ext[number].at[pl.ds((kind + 1) * owned, owned)],
            send_sem=own_send.at[number, kind],
            recv_sem=own_recv.at[number, kind],
            device_id={"nodes": target},
            device_id_type=MESH,
        )

    relayed = jnp.where(core == odd, 2, 3)
    to_mate = [block_copy(n, 0, 0, mate) for n in range(count)]
    to_partner = [block_copy(n, 1, 0, partner) for n in range(count)]
    forward = [block_copy(n, 2, 2, onward) for n in range(count)]
    relay = [block_copy(n, 3, relayed, mate) for n in range(count)]

    to_partner[0].start()
    list_copies = []
    for column, offset in enumerate((1, -1, 2, -2)):
        copy = pltpu.make_async_remote_copy(
            src_ref=list_ref,
            dst_ref=lists.at[column],
            send_sem=list_send.at[column],
            recv_sem=list_recv.at[column],
            device_id={"nodes": lax.rem(me + offset + size, size)},
            device_id_type=MESH,
        )
        copy.start()
        list_copies.append(copy)

    def pool_copy(step):
        return pltpu.make_async_remote_copy(
            src_ref=pooled.at[me],
            dst_ref=pooled.at[me],
            send_sem=pool_send.at[step],
            recv_sem=pool_recv.at[step],
            device_id={"nodes": lax.rem(me + step, size)},
            device_id_type=MESH,
        )

    def pool_arrival(step):
        return pltpu.make_async_remote_copy(
            src_ref=pooled.at[me],
            dst_ref=pooled.at[lax.rem(me - step + size, size)],
            send_sem=pool_send.at[step],
            recv_sem=pool_recv.at[step],
            device_id={"nodes": lax.rem(me + step, size)},
            device_id_type=MESH,
        )

    def send_pooled(step, carry):
        pool_copy(step).start()
        return carry

    lax.fori_loop(1, size, send_pooled, 0)
    for copy in to_partner[1:] + to_mate:
        copy.start()

    live = edge_count[0]

    def panel(slot, carry):
        block = matrix[slot]
        at = pl.ds(pl.multiple_of(slot * BLOCK, BLOCK), BLOCK)
        for owner in range(owned):
            use = jnp.where((edge_dst[0, slot] == owner) & (slot < live), 1.0, 0.0)
            weights[owner * BLOCK : (owner + 1) * BLOCK, at] = (block * use).astype(jnp.bfloat16)
        return carry

    lax.fori_loop(0, slots, panel, 0)

    for copy in list_copies:
        copy.wait()
    to_scalar = pltpu.make_async_copy(lists, lists_scalar, local_sem)
    to_scalar.start()
    to_scalar.wait()

    behind_one = jnp.where(core == 1, 1, 4)
    ahead_one = jnp.where(core == 0, 1, 4)
    behind_two = jnp.where(odd == 0, 3, 2)
    ahead_two = jnp.where(odd == 0, 2, 3)

    def place(slot):
        source = edge_src[0, slot]
        away = jnp.maximum(source - owned, 0)
        column = away // 2
        base = jnp.where(
            column == 0,
            behind_one,
            jnp.where(column == 1, ahead_one, jnp.where(column == 2, behind_two, ahead_two)),
        )
        block = lists_scalar[column, 0, away]
        return jnp.where(source < owned, source, base * owned + block)

    def wait_pooled(step, carry):
        pool_arrival(step).wait()
        return carry

    def combine(number):
        start, width, wide = pieces[number]
        buffer = ext[number]

        def pick(slot, carry):
            at = pl.ds(pl.multiple_of(slot * BLOCK, BLOCK), BLOCK)
            gathered[at, :wide] = buffer[place(slot)]
            return carry

        lax.fori_loop(0, slots, pick, 0)
        if number == 0:
            lax.fori_loop(1, size, wait_pooled, 0)
        every = pooled[...].reshape(-1, PIECE)
        mixed = jnp.dot(mixing[number], every, preferred_element_type=jnp.float32)
        for owner in range(owned):
            coarse[owner] = jnp.broadcast_to(mixed[owner : owner + 1], (8, PIECE))

        def rows_of(owner, carry):
            at = pl.ds(pl.multiple_of(owner * BLOCK, BLOCK), BLOCK)
            moved = jnp.dot(
                weights[at, :], gathered[:, :wide], preferred_element_type=jnp.float32
            )
            lifted = columns[at, 1:2] * coarse[owner][0:1, :width]
            field[at, start : start + width] = (
                state[at, start : start + width] + moved[:, :width] + lifted
            )
            return carry

        lax.fori_loop(0, owned, rows_of, 0)

    for number in range(count + 1):
        if number < count:
            to_partner[number].wait()
            forward[number].start()
        if number >= 1:
            forward[number - 1].wait()
            relay[number - 1].start()
            to_mate[number - 1].wait()
            relay[number - 1].wait()
            combine(number - 1)


def network_kernel(field, gain, proj_in, proj_out, out):
    flat = field[...]
    mean_square = jnp.mean(flat * flat, axis=1, keepdims=True)
    normed = (flat * lax.rsqrt(mean_square + 1e-06) * gain[...]).astype(jnp.bfloat16)
    pre_act = jnp.dot(normed, proj_in[...], preferred_element_type=jnp.float32)
    hidden = jax.nn.gelu(pre_act).astype(jnp.bfloat16)
    out[...] = flat + jnp.dot(hidden, proj_out[...], preferred_element_type=jnp.float32)


def shards(
    size,
    wave_state,
    pool_weight,
    lift_weight,
    coarse_matrix,
    block_matrix,
    edge_dst,
    edge_src,
    edge_count,
    send_list,
    norm_gain,
    proj_in,
    proj_out,
):
    nodes, bins = wave_state.shape
    owned = nodes // BLOCK
    slots = edge_src.shape[1]
    pieces = pieces_of(bins)
    count = len(pieces)
    position = lax.axis_index("nodes")
    mine = lax.dynamic_slice_in_dim(coarse_matrix, position * owned, owned, 0)
    mine = mine.reshape(1, owned, size, 1, owned)
    same = jnp.eye(count, dtype=jnp.bfloat16).reshape(count, 1, 1, count, 1)
    mixing = (mine * same).reshape(count, owned, size * count * owned)
    mixing = jnp.pad(mixing, ((0, 0), (0, 16 - owned), (0, 0)))
    columns = jnp.stack([pool_weight, lift_weight], axis=1)
    lists = jnp.pad(send_list.reshape(1, -1), ((0, 7), (0, 120)))

    vmem = pl.BlockSpec(memory_space=pltpu.VMEM)
    smem = pl.BlockSpec(memory_space=pltpu.SMEM)
    field = pl.pallas_call(
        functools.partial(exchange_kernel, size, owned, pieces),
        out_shape=jax.ShapeDtypeStruct((nodes, bins), jnp.float32),
        in_specs=[vmem, vmem, vmem, vmem, smem, smem, smem, vmem],
        out_specs=vmem,
        scratch_shapes=[
            pltpu.VMEM((nodes, slots * BLOCK), jnp.bfloat16),
            pltpu.VMEM((slots * BLOCK, PIECE), jnp.bfloat16),
            pltpu.VMEM((size, count * owned, PIECE), jnp.bfloat16),
            pltpu.VMEM((4, 8, 128), jnp.int32),
            pltpu.SMEM((4, 8, 128), jnp.int32),
            pltpu.VMEM((owned, 8, PIECE), jnp.float32),
            pltpu.SemaphoreType.DMA((count, 4)),
            pltpu.SemaphoreType.DMA((count, 4)),
            pltpu.SemaphoreType.DMA((4,)),
            pltpu.SemaphoreType.DMA((4,)),
            pltpu.SemaphoreType.DMA((size,)),
            pltpu.SemaphoreType.DMA((size,)),
            pltpu.SemaphoreType.DMA,
        ]
        + [pltpu.VMEM((5 * owned, BLOCK, wide), jnp.bfloat16) for _, _, wide in pieces],
        compiler_params=pltpu.CompilerParams(
            collective_id=0, has_side_effects=True, vmem_limit_bytes=40 * 2**20
        ),
        name="exchange",
    )(wave_state, columns, mixing, block_matrix[0], edge_dst, edge_src, edge_count, lists)

    tile = min(256, nodes)
    hidden_size = proj_in.shape[1]
    return pl.pallas_call(
        network_kernel,
        grid=(nodes // tile,),
        out_shape=jax.ShapeDtypeStruct((nodes, bins), jnp.float32),
        in_specs=[
            pl.BlockSpec((tile, bins), lambda i: (i, 0)),
            pl.BlockSpec((1, bins), lambda i: (0, 0)),
            pl.BlockSpec((bins, hidden_size), lambda i: (0, 0)),
            pl.BlockSpec((hidden_size, bins), lambda i: (0, 0)),
        ],
        out_specs=pl.BlockSpec((tile, bins), lambda i: (i, 0)),
        compiler_params=pltpu.CompilerParams(vmem_limit_bytes=40 * 2**20),
        name="network",
    )(field, norm_gain.reshape(1, bins), proj_in, proj_out)


def solution(mesh):
    in_specs = (
        P(("members", "nodes"), None),
        P("nodes"),
        P("nodes"),
        P(),
        P("nodes", None, None, None),
        P("nodes", None),
        P("nodes", None),
        P("nodes"),
        P("nodes", None, None),
        P(),
        P(),
        P(),
    )
    out_specs = P(("members", "nodes"), None)
    return jax.shard_map(
        functools.partial(shards, mesh.shape["nodes"]),
        mesh=mesh,
        in_specs=in_specs,
        out_specs=out_specs,
        check_vma=False,
    )
```

time: 210 us -> 81.3 us (0.39)
  Pallas kernels: 0 us -> 59.9 us
  blocking collectives: 57.5 us -> 0 us
  local copies, waits for them, and re-layouts: 69.7 us -> 19.4 us
  matrix products: 46.5 us -> 0 us
  other arithmetic: 23.1 us -> 0.72 us
  starting transfers between devices: 10.2 us -> 0 us
    pallas_call x0 -> x2, Pallas kernels: none -> 59.9 us  [the longest x1 55.9 us: shards(): pl.pallas_call(functools.partial(exchange_kernel, size, owned, pieces), o...]
    all_gather x1 -> x0, blocking collectives: 57.5 us -> none  [shards(): lax.all_gather(pooled, 'nodes', axis=0, tiled=True)]
    dot_general x5 -> x0, matrix products: 46.5 us -> none  [the longest x1 18.1 us: shards(): jnp.einsum('ne,eib->nib', selector, product, precision=lax.Precision.HIGH...]
    concatenate x2 -> x0, local copies, waits for them, and re-layouts: 36.1 us -> none  [shards(): extended = jnp.concatenate([blocks_own] + arrived, 0)]
    gather x5 -> x0, local copies, waits for them, and re-layouts: 24.9 us -> none  [the longest x4 13.9 us: shards(): jnp.take(blocks_own, chosen[column], axis=0)]
    select_n x9 -> x0, other arithmetic: 23 us -> none  [the longest x8 23 us: shards(): jnp.take(blocks_own, chosen[column], axis=0)]
    unnamed x15 -> x19, local copies, waits for them, and re-layouts: 0.11 us -> 15.9 us
    ppermute x4 -> x0, starting transfers between devices: 10.2 us -> none  [from_behind(): lax.ppermute(shard, axis, [(i, (i + by) % size) for i in range(size)])]
  transfers between devices with their start and end apart: 4 -> 0, of which waited for: 0 -> 0; matrix products, arithmetic and copies ran while one was open for 18% -> 0% of each run, Pallas kernels for 0% -> 0%
where the time goes in v2:
time: 81.3 us; the launch traced here: 80.8 us
  Pallas kernels  59.9 us (74%)
  local copies, waits for them, and re-layouts  19.4 us (24%)
    pallas_call x1, Pallas kernels, shards(): pl.pallas_call(functools.partial(exchange_kernel, size, owned, pieces), o...  55.9 us
    unnamed x19, local copies, waits for them, and re-layouts  15.9 us
    pallas_call x1, Pallas kernels, shards(): pl.pallas_call(network_kernel, grid=(nodes // tile,), out_shape=jax.Shape...  4.06 us
    pallas_call x1, local copies, waits for them, and re-layouts, shards(): pl.pallas_call(network_kernel, grid=(nodes // tile,), out_shape=jax.Shape...  2.12 us

profile of v2, /device:TPU:0, one launch (start us, length us, event | category | flops | bytes accessed | tf_op | source)
XLA Modules:
  0.0 80.8 jit_solution(5214710758627007521)
XLA Ops:
  0.0 0.0 copy-start
  0.7 0.1 copy-done
  0.7 0.8 copy.23
  1.5 0.1 reshape.20
  1.6 0.7 pad_maximum_fusion
  2.3 0.7 reshape.21.gain
  3.0 0.1 mul.28
  3.1 0.1 mul.30
  3.3 0.1 mul.32
  3.4 0.1 mul.33
  3.5 0.1 copy.25.columns
  3.7 0.0 copy-start.6
  3.7 0.0 copy-start.7
  3.7 2.2 %copy.24.state = f32[512,1296]{1,0:T(8,128)S(1)} copy(f32[512,1296]{0,1:T(8,128)} %param.12) | data formatting | bytes 5308416 | tf_op args[0]
  6.0 0.0 copy-done.6
  6.0 0.0 copy-done.7
  6.0 0.0 copy-start.5
  6.0 1.3 %copy-done.5 = f32[1,20,128,128]{3,2,1,0:T(8,128)S(1)} copy-done((f32[1,20,128,128]{3,2,1,0:T(8,128)S(1)}, f32[1,20,128,128]{3,2,1,0:T(8,128)}, u32[]{:S(2)}) %copy-start.5) | copy-done | bytes 1310744
  7.3 55.9 %exchange.1.field = f32[512,1296]{1,0:T(8,128)S(1)} custom-call(f32[512,1296]{1,0:T(8,128)S(1)} %copy.24.state, f32[512,2]{1,0:T(8,128)S(1)} %copy.25.columns, bf16[4,16,256]{2,1,0:T(8,128)(2,1)S(1)} %pad.8.mixing, f32[20,128,128]{2,1,0:T(8,128)S(1)} %bitcast.3, s32[1,20]{1,0:T(1,128)S(1)} %copy-done.6, s32[1,20]{1,0:T(1,128)S(1)} %copy-done.7, ...), custom_call_target="tpu_custom_call" | custom-call | tf_op jit(solution)/shard_map/exchange/pallas_call | solution.py:247
  63.2 0.0 copy-start.1
  63.2 1.6 %copy-done.1 = f32[512,1296]{1,0:T(8,128)} copy-done((f32[512,1296]{1,0:T(8,128)}, f32[512,1296]{1,0:T(8,128)S(1)}, u32[]{:S(2)}) %copy-start.1) | copy-done | bytes 2654232
  64.7 4.5 %copy.26.proj_out = bf16[1024,1296]{1,0:T(8,128)(2,1)} copy(bf16[1024,1296]{0,1:T(8,128)(2,1)} %param.23) | data formatting | bytes 5308416 | tf_op args[11]
  69.2 0.0 copy-start.2
  69.3 1.8 %copy-done.2 = f32[512,1296]{1,0:T(8,128)S(1)} copy-done((f32[512,1296]{1,0:T(8,128)S(1)}, f32[512,1296]{1,0:T(8,128)}, u32[]{:S(2)}) %copy-start.2) | copy-done | bytes 2654232
  71.1 0.0 copy-start.3
  71.1 1.8 %copy-done.3 = bf16[1024,1296]{1,0:T(8,128)(2,1)S(1)} copy-done((bf16[1024,1296]{1,0:T(8,128)(2,1)S(1)}, bf16[1024,1296]{1,0:T(8,128)(2,1)}, u32[]{:S(2)}) %copy-start.3) | copy-done | bytes 2654232
  72.9 0.0 copy-start.4
  72.9 1.7 %copy-done.4 = bf16[1296,1024]{1,0:T(8,128)(2,1)S(1)} copy-done((bf16[1296,1024]{1,0:T(8,128)(2,1)S(1)}, bf16[1296,1024]{1,0:T(8,128)(2,1)}, u32[]{:S(2)}) %copy-start.4) | copy-done | bytes 2654232
  74.6 4.1 %network.1 = f32[512,1296]{1,0:T(8,128)S(1)} custom-call(f32[512,1296]{1,0:T(8,128)S(1)} %copy-done.2, f32[1,1296]{1,0:T(1,128)S(1)} %reshape.21.gain, bf16[1296,1024]{1,0:T(8,128)(2,1)S(1)} %copy-done.4, bf16[1024,1296]{1,0:T(8,128)(2,1)S(1)} %copy-done.3), custom_call_target="tpu_custom_call" | custom-call | tf_op jit(solution)/shard_map/network/pallas_call | solution.py:276
  78.7 2.1 %copy.27 = f32[512,1296]{0,1:T(8,128)} copy(f32[512,1296]{1,0:T(8,128)S(1)} %network.1) | data formatting | bytes 5308416 | tf_op jit(solution)/shard_map/network/pallas_call | solution.py:276
  (6 shorter events, 0.1 us)
Async XLA Ops:
  0.0 0.7 copy-start
  3.7 2.3 %copy-start.6 = (s32[1,20]{1,0:T(1,128)S(1)}, s32[1,20]{1,0:T(1,128)}, u32[]{:S(2)}) copy-start(s32[1,20]{1,0:T(1,128)} %edge_dst.1) | copy-start | bytes 244
  3.7 2.3 %copy-start.7 = (s32[1,20]{1,0:T(1,128)S(1)}, s32[1,20]{1,0:T(1,128)}, u32[]{:S(2)}) copy-start(s32[1,20]{1,0:T(1,128)} %edge_src.1) | copy-start | bytes 244
  6.0 1.3 %copy-start.5 = (f32[1,20,128,128]{3,2,1,0:T(8,128)S(1)}, f32[1,20,128,128]{3,2,1,0:T(8,128)}, u32[]{:S(2)}) copy-start(f32[1,20,128,128]{3,2,1,0:T(8,128)} %param.16) | copy-start | bytes 3932164
  63.2 1.6 %copy-start.1 = (f32[512,1296]{1,0:T(8,128)}, f32[512,1296]{1,0:T(8,128)S(1)}, u32[]{:S(2)}) copy-start(f32[512,1296]{1,0:T(8,128)S(1)} %exchange.1.field) | copy-start | bytes 7962628
  69.2 1.8 %copy-start.2 = (f32[512,1296]{1,0:T(8,128)S(1)}, f32[512,1296]{1,0:T(8,128)}, u32[]{:S(2)}) copy-start(f32[512,1296]{1,0:T(8,128)} %copy-done.1) | copy-start | bytes 7962628
  71.1 1.8 %copy-start.3 = (bf16[1024,1296]{1,0:T(8,128)(2,1)S(1)}, bf16[1024,1296]{1,0:T(8,128)(2,1)}, u32[]{:S(2)}) copy-start(bf16[1024,1296]{1,0:T(8,128)(2,1)} %copy.26.proj_out) | copy-start | bytes 7962628
  72.9 1.7 %copy-start.4 = (bf16[1296,1024]{1,0:T(8,128)(2,1)S(1)}, bf16[1296,1024]{1,0:T(8,128)(2,1)}, u32[]{:S(2)}) copy-start(bf16[1296,1024]{1,0:T(8,128)(2,1)} %proj_in.1) | copy-start | bytes 7962628

commit v3 on v2

v3 whole, which is shorter than its diff:
```python
import functools

import jax
import jax.numpy as jnp
from jax import lax
from jax.experimental import pallas as pl
from jax.experimental.pallas import tpu as pltpu
from jax.sharding import PartitionSpec as P

BLOCK = 128
PIECE = 384
CHUNK = 144
MESH = pl.DeviceIdType.MESH


def exchange_kernel(
    size, owned, chunk, pieces,
    state, pool, lift, mixing, matrix, edge_dst, edge_src, edge_count, list_ref, gain_row, proj_in_hbm, proj_out_hbm,
    out,
    weights, gathered, pooled, lists, lists_scalar, coarse, gain, proj_in, proj_in_turned, proj_out,
    own_send, own_recv, list_send, list_recv, pool_send, pool_recv, local_sem,
    *ext,
):
    bins, nodes = state.shape
    slots = matrix.shape[0]
    count = len(ext)
    me = lax.axis_index("nodes")
    core = lax.rem(me, 2)
    chip = me // 2
    odd = lax.rem(chip, 2)
    mate = chip * 2 + 1 - core
    partner = (chip + 1 - 2 * odd) * 2 + core
    onward = lax.rem(me + 4 - 8 * odd + size, size)

    barrier = pltpu.get_barrier_semaphore()

    def greet(step, carry):
        pl.semaphore_signal(
            barrier, inc=1, device_id={"nodes": lax.rem(me + step, size)}, device_id_type=MESH
        )
        return carry

    lax.fori_loop(1, size, greet, 0)
    fetch_in = pltpu.make_async_copy(proj_in_hbm, proj_in, local_sem.at[1])
    fetch_out = pltpu.make_async_copy(proj_out_hbm, proj_out, local_sem.at[2])
    fetch_in.start()
    fetch_out.start()

    for number in range(count):
        for block in range(owned):
            part = state[number * chunk : (number + 1) * chunk, block * BLOCK : (block + 1) * BLOCK]
            ext[number][block] = part.astype(jnp.bfloat16)

    pl.semaphore_wait(barrier, size - 1)

    def block_copy(number, kind, source, target):
        return pltpu.make_async_remote_copy(
            src_ref=ext[number].at[pl.ds(source * owned, owned)],
            dst_ref=ext[number].at[pl.ds((kind + 1) * owned, owned)],
            send_sem=own_send.at[number, kind],
            recv_sem=own_recv.at[number, kind],
            device_id={"nodes": target},
            device_id_type=MESH,
        )

    relayed = jnp.where(core == odd, 2, 3)
    to_mate = [block_copy(n, 0, 0, mate) for n in range(count)]
    to_partner = [block_copy(n, 1, 0, partner) for n in range(count)]
    forward = [block_copy(n, 2, 2, onward) for n in range(count)]
    relay = [block_copy(n, 3, relayed, mate) for n in range(count)]

    to_partner[0].start()
    to_partner[1].start()
    list_copies = []
    for column, offset in enumerate((1, -1, 2, -2)):
        copy = pltpu.make_async_remote_copy(
            src_ref=list_ref,
            dst_ref=lists.at[column],
            send_sem=list_send.at[column],
            recv_sem=list_recv.at[column],
            device_id={"nodes": lax.rem(me + offset + size, size)},
            device_id_type=MESH,
        )
        copy.start()
        list_copies.append(copy)

    row_id = lax.broadcasted_iota(jnp.int32, (16, nodes), 0)
    node_block = lax.broadcasted_iota(jnp.int32, (16, nodes), 1) // BLOCK
    pooling = jnp.where(row_id == node_block, jnp.broadcast_to(pool[...], (16, nodes)), 0.0)
    rows = []
    for start, width in pieces:
        part = lax.dot_general(
            pooling,
            state[start : start + width, :],
            (((1,), (1,)), ((), ())),
            precision=lax.Precision.HIGHEST,
            preferred_element_type=jnp.float32,
        )[:owned]
        if width < PIECE:
            part = jnp.concatenate([part, jnp.zeros((owned, PIECE - width), jnp.float32)], 1)
        rows.append(part)
    pooled[me] = jnp.concatenate(rows, 0).astype(jnp.bfloat16)

    def pool_copy(step, row):
        return pltpu.make_async_remote_copy(
            src_ref=pooled.at[me],
            dst_ref=pooled.at[row],
            send_sem=pool_send.at[step],
            recv_sem=pool_recv.at[step],
            device_id={"nodes": lax.rem(me + step, size)},
            device_id_type=MESH,
        )

    def send_pooled(step, carry):
        pool_copy(step, me).start()
        return carry

    lax.fori_loop(1, size, send_pooled, 0)
    for copy in to_partner[2:] + to_mate:
        copy.start()

    live = edge_count[0]

    def panel(slot, carry):
        block = matrix[slot].T
        at = pl.ds(pl.multiple_of(slot * BLOCK, BLOCK), BLOCK)
        for owner in range(owned):
            use = jnp.where((edge_dst[0, slot] == owner) & (slot < live), 1.0, 0.0)
            weights[at, owner * BLOCK : (owner + 1) * BLOCK] = (block * use).astype(jnp.bfloat16)
        return carry

    lax.fori_loop(0, slots, panel, 0)

    for copy in list_copies:
        copy.wait()
    to_scalar = pltpu.make_async_copy(lists, lists_scalar, local_sem.at[0])
    to_scalar.start()
    to_scalar.wait()

    behind_one = jnp.where(core == 1, 1, 4)
    ahead_one = jnp.where(core == 0, 1, 4)
    behind_two = jnp.where(odd == 0, 3, 2)
    ahead_two = jnp.where(odd == 0, 2, 3)

    def place(slot):
        source = edge_src[0, slot]
        away = jnp.maximum(source - owned, 0)
        column = away // 2
        base = jnp.where(
            column == 0,
            behind_one,
            jnp.where(column == 1, ahead_one, jnp.where(column == 2, behind_two, ahead_two)),
        )
        block = lists_scalar[column, 0, away]
        return jnp.where(source < owned, source, base * owned + block)

    def wait_pooled(step, carry):
        pool_copy(step, lax.rem(me - step + size, size)).wait()
        return carry

    def mix():
        lax.fori_loop(1, size, wait_pooled, 0)
        every = pooled[...].reshape(-1, PIECE)
        for number, (start, width) in enumerate(pieces):
            mixed = jnp.dot(mixing[number], every, preferred_element_type=jnp.float32)
            mixed = jnp.concatenate([mixed, jnp.zeros((BLOCK - 16, PIECE), jnp.float32)], 0)
            coarse[start : start + width, :] = mixed.T[:width]

    def turn():
        spread = jnp.broadcast_to(gain_row[...], (BLOCK, gain_row.shape[1]))
        gain[...] = spread.T[:bins]
        fetch_in.wait()
        for at in range(0, proj_in.shape[1], BLOCK):
            proj_in_turned[at : at + BLOCK, :] = proj_in[:, at : at + BLOCK].T

    def combine(number):
        buffer = ext[number]
        at_bins = slice(number * chunk, (number + 1) * chunk)

        def pick(slot, carry):
            at = pl.ds(pl.multiple_of(slot * BLOCK, BLOCK), BLOCK)
            gathered[:, at] = buffer[place(slot)]
            return carry

        lax.fori_loop(0, slots, pick, 0)
        moved = jnp.dot(gathered[...], weights[...], preferred_element_type=jnp.float32)
        for owner in range(owned):
            own = slice(owner * BLOCK, (owner + 1) * BLOCK)
            lifted = coarse[at_bins, owner : owner + 1] * lift[0:1, own]
            out[at_bins, own] = state[at_bins, own] + moved[:, own] + lifted

    for number in range(count + 2):
        if number < count:
            to_partner[number].wait()
            forward[number].start()
        if 1 <= number <= count:
            forward[number - 1].wait()
            relay[number - 1].start()
        if number == 1:
            mix()
            turn()
        if number >= 2:
            to_mate[number - 2].wait()
            relay[number - 2].wait()
            combine(number - 2)

    fetch_out.wait()
    tile = 2 * BLOCK

    def network(step, carry):
        at = pl.ds(pl.multiple_of(step * tile, tile), tile)
        flat = out[:, at]
        mean_square = jnp.mean(flat * flat, axis=0, keepdims=True)
        wide_gain = jnp.concatenate([gain[...]] * 2, 1)
        normed = (flat * lax.rsqrt(mean_square + 1e-06) * wide_gain).astype(jnp.bfloat16)
        pre_act = jnp.dot(proj_in_turned[...], normed, preferred_element_type=jnp.float32)
        hidden = jax.nn.gelu(pre_act).astype(jnp.bfloat16)
        out[:, at] = out[:, at] + jnp.dot(proj_out[...], hidden, preferred_element_type=jnp.float32)
        return carry

    lax.fori_loop(0, nodes // tile, network, 0)


def shards(
    size,
    wave_state,
    pool_weight,
    lift_weight,
    coarse_matrix,
    block_matrix,
    edge_dst,
    edge_src,
    edge_count,
    send_list,
    norm_gain,
    proj_in,
    proj_out,
):
    nodes, bins = wave_state.shape
    owned = nodes // BLOCK
    slots = edge_src.shape[1]
    hidden_size = proj_in.shape[1]
    pieces = [(start, min(PIECE, bins - start)) for start in range(0, bins, PIECE)]
    count = len(pieces)
    chunk = CHUNK
    chunks = bins // chunk
    position = lax.axis_index("nodes")
    mine = lax.dynamic_slice_in_dim(coarse_matrix, position * owned, owned, 0)
    mine = mine.reshape(1, owned, size, 1, owned)
    same = jnp.eye(count, dtype=jnp.bfloat16).reshape(count, 1, 1, count, 1)
    mixing = (mine * same).reshape(count, owned, size * count * owned)
    mixing = jnp.pad(mixing, ((0, 0), (0, 16 - owned), (0, 0)))
    lists = jnp.pad(send_list.reshape(1, -1), ((0, 7), (0, 120)))
    gain_row = jnp.pad(norm_gain, (0, -bins % BLOCK)).reshape(1, -1)

    vmem = pl.BlockSpec(memory_space=pltpu.VMEM)
    smem = pl.BlockSpec(memory_space=pltpu.SMEM)
    anywhere = pl.BlockSpec(memory_space=pl.ANY)
    turned = pl.pallas_call(
        functools.partial(exchange_kernel, size, owned, chunk, pieces),
        out_shape=jax.ShapeDtypeStruct((bins, nodes), jnp.float32),
        in_specs=[vmem] * 5 + [smem] * 3 + [vmem] * 2 + [anywhere] * 2,
        out_specs=vmem,
        scratch_shapes=[
            pltpu.VMEM((slots * BLOCK, nodes), jnp.bfloat16),
            pltpu.VMEM((chunk, slots * BLOCK), jnp.bfloat16),
            pltpu.VMEM((size, count * owned, PIECE), jnp.bfloat16),
            pltpu.VMEM((4, 8, 128), jnp.int32),
            pltpu.SMEM((4, 8, 128), jnp.int32),
            pltpu.VMEM((bins, BLOCK), jnp.float32),
            pltpu.VMEM((bins, BLOCK), jnp.float32),
            pltpu.VMEM((bins, hidden_size), jnp.bfloat16),
            pltpu.VMEM((hidden_size, bins), jnp.bfloat16),
            pltpu.VMEM((bins, hidden_size), jnp.bfloat16),
            pltpu.SemaphoreType.DMA((chunks, 4)),
            pltpu.SemaphoreType.DMA((chunks, 4)),
            pltpu.SemaphoreType.DMA((4,)),
            pltpu.SemaphoreType.DMA((4,)),
            pltpu.SemaphoreType.DMA((size,)),
            pltpu.SemaphoreType.DMA((size,)),
            pltpu.SemaphoreType.DMA((3,)),
        ]
        + [pltpu.VMEM((5 * owned, chunk, BLOCK), jnp.bfloat16)] * chunks,
        compiler_params=pltpu.CompilerParams(
            collective_id=0, has_side_effects=True, vmem_limit_bytes=48 * 2**20
        ),
        name="exchange",
    )(
        wave_state.T,
        pool_weight.reshape(1, nodes),
        lift_weight.reshape(1, nodes),
        mixing,
        block_matrix[0],
        edge_dst,
        edge_src,
        edge_count,
        lists,
        gain_row,
        proj_in,
        proj_out.T,
    )
    return turned.T


def solution(mesh):
    in_specs = (
        P(("members", "nodes"), None),
        P("nodes"),
        P("nodes"),
        P(),
        P("nodes", None, None, None),
        P("nodes", None),
        P("nodes", None),
        P("nodes"),
        P("nodes", None, None),
        P(),
        P(),
        P(),
    )
    out_specs = P(("members", "nodes"), None)
    return jax.shard_map(
        functools.partial(shards, mesh.shape["nodes"]),
        mesh=mesh,
        in_specs=in_specs,
        out_specs=out_specs,
        check_vma=False,
    )
```

time: 81.3 us -> 68.6 us (0.84)
  local copies, waits for them, and re-layouts: 19.4 us -> 7.61 us
    unnamed x19 -> x14, local copies, waits for them, and re-layouts: 15.9 us -> 6.33 us
    pallas_call x1 -> x0, local copies, waits for them, and re-layouts: 2.12 us -> none  [shards(): pl.pallas_call(network_kernel, grid=(nodes // tile,), out_shape=jax.Shape...]
    pallas_call x2 -> x1, Pallas kernels: 59.9 us -> 59.9 us  [shards(): pl.pallas_call(functools.partial(exchange_kernel, size, owned, chunk, pie...]
where the time goes in v3:
time: 68.6 us; the launch traced here: 68.2 us
  Pallas kernels  59.9 us (87%)
  local copies, waits for them, and re-layouts  7.61 us (11%)
  between operations  0.72 us (1%)
    pallas_call x1, Pallas kernels, shards(): pl.pallas_call(functools.partial(exchange_kernel, size, owned, chunk, pie...  59.9 us
    unnamed x14, local copies, waits for them, and re-layouts  6.33 us

profile of v3, /device:TPU:0, one launch (start us, length us, event | category | flops | bytes accessed | tf_op | source)
XLA Modules:
  0.0 68.2 jit_solution(10050127859938465658)
XLA Ops:
  0.0 0.0 copy-start
  0.7 0.1 copy-done
  0.7 0.8 %copy.14 = s32[1,4,2]{2,1,0:T(4,128)S(1)} copy(s32[1,4,2]{1,2,0:T(2,128)} %param.20) | data formatting | bytes 64 | tf_op args[8]
  1.5 0.1 reshape.28
  1.6 0.7 %pad.14 = f32[1408]{0:T(1024)S(1)} pad(f32[1296]{0:T(1024)} %param.21, f32[]{:T(128)} %constant.13.clone.1), padding=0_112 | pad | bytes 10820 | tf_op jit(solution)/shard_map/jit(_pad)/pad | solution.py:254
  2.3 0.1 mul.28
  2.4 0.1 mul.30
  2.6 0.1 mul.32
  2.7 0.1 mul.33
  2.8 0.0 copy-start.1
  2.8 1.3 %copy-done.1 = f32[1,20,128,128]{3,2,1,0:T(8,128)S(1)} copy-done((f32[1,20,128,128]{3,2,1,0:T(8,128)S(1)}, f32[1,20,128,128]{3,2,1,0:T(8,128)}, u32[]{:S(2)}) %copy-start.1) | copy-done | bytes 1310744
  4.2 0.0 copy-start.2
  4.2 0.7 copy-done.2
  4.8 0.0 copy-start.3
  4.8 0.7 copy-done.3
  5.5 0.0 copy-start.4
  5.5 0.7 copy-done.4
  6.2 0.0 copy-start.5
  6.2 0.7 copy-done.5
  6.8 59.9 %exchange.1 = f32[1296,512]{1,0:T(8,128)S(1)} custom-call(f32[1296,512]{1,0:T(8,128)} %bitcast.10, f32[1,512]{1,0:T(1,128)S(1)} %bitcast.8, f32[1,512]{1,0:T(1,128)S(1)} %bitcast.9, bf16[4,16,256]{2,1,0:T(8,128)(2,1)S(1)} %pad.12.mixing, f32[20,128,128]{2,1,0:T(8,128)S(1)} %bitcast.7, s32[1,20]{1,0:T(1,128)S(1)} %copy-done.4, s32[1,20]{1,0:T(1,128)S(1)} %copy-done.5, ...), custom_call_target="tpu_custom_call" | custom-call | tf_op jit(solution)/shard_map/exchange/pallas_call | solution.py:259
  66.7 1.5 %copy.17 = f32[512,1296]{0,1:T(8,128)} copy(f32[512,1296]{0,1:T(8,128)S(1)} %bitcast.6) | data formatting | bytes 5308416
  (7 shorter events, 0.1 us)
Async XLA Ops:
  0.0 0.7 %copy-start = (bf16[64,64]{1,0:T(8,128)(2,1)S(1)}, bf16[64,64]{1,0:T(8,128)(2,1)}, u32[]{:S(2)}) copy-start(bf16[64,64]{1,0:T(8,128)(2,1)} %param.15) | copy-start | bytes 24580
  2.8 1.3 %copy-start.1 = (f32[1,20,128,128]{3,2,1,0:T(8,128)S(1)}, f32[1,20,128,128]{3,2,1,0:T(8,128)}, u32[]{:S(2)}) copy-start(f32[1,20,128,128]{3,2,1,0:T(8,128)} %param.16) | copy-start | bytes 3932164
  4.2 0.7 copy-start.2
  4.8 0.7 copy-start.3
  5.5 0.7 copy-start.4
  6.2 0.7 copy-start.5

commit v4 on v3

--- a/solution.py
+++ b/solution.py
@@ -15,8 +15,10 @@
 
 def exchange_kernel(
     size, owned, chunk, pieces,
-    state, pool, lift, mixing, matrix, edge_dst, edge_src, edge_count, list_ref, gain_row, proj_in_hbm, proj_out_hbm,
+    state, pool_hbm, lift_hbm, mixing, matrix_hbm, edge_dst_hbm, edge_src_hbm, edge_count, list_ref, gain_row,
+    proj_in_hbm, proj_out_hbm,
     out,
+    pool, lift, matrix, edge_dst, edge_src,
     weights, gathered, pooled, lists, lists_scalar, coarse, gain, proj_in, proj_in_turned, proj_out,
     own_send, own_recv, list_send, list_recv, pool_send, pool_recv, local_sem,
     *ext,
@@ -43,8 +45,20 @@
     lax.fori_loop(1, size, greet, 0)
     fetch_in = pltpu.make_async_copy(proj_in_hbm, proj_in, local_sem.at[1])
     fetch_out = pltpu.make_async_copy(proj_out_hbm, proj_out, local_sem.at[2])
-    fetch_in.start()
-    fetch_out.start()
+    fetch_small = [
+        pltpu.make_async_copy(source, target, local_sem.at[3 + number])
+        for number, (source, target) in enumerate(
+            [
+                (pool_hbm, pool),
+                (lift_hbm, lift),
+                (edge_dst_hbm, edge_dst),
+                (edge_src_hbm, edge_src),
+                (matrix_hbm, matrix),
+            ]
+        )
+    ]
+    for copy in fetch_small + [fetch_in, fetch_out]:
+        copy.start()
 
     for number in range(count):
         for block in range(owned):
@@ -83,6 +97,9 @@
         )
         copy.start()
         list_copies.append(copy)
+
+    for copy in fetch_small:
+        copy.wait()
 
     row_id = lax.broadcasted_iota(jnp.int32, (16, nodes), 0)
     node_block = lax.broadcasted_iota(jnp.int32, (16, nodes), 1) // BLOCK
@@ -166,12 +183,15 @@
             mixed = jnp.concatenate([mixed, jnp.zeros((BLOCK - 16, PIECE), jnp.float32)], 0)
             coarse[start : start + width, :] = mixed.T[:width]
 
-    def turn():
+    def turn_gain():
         spread = jnp.broadcast_to(gain_row[...], (BLOCK, gain_row.shape[1]))
         gain[...] = spread.T[:bins]
-        fetch_in.wait()
-        for at in range(0, proj_in.shape[1], BLOCK):
-            proj_in_turned[at : at + BLOCK, :] = proj_in[:, at : at + BLOCK].T
+
+    def turn(part):
+        at = slice(part * BLOCK, (part + 1) * BLOCK)
+        proj_in_turned[at, :] = proj_in[:, at].T
+
+    parts = proj_in.shape[1] // BLOCK
 
     def combine(number):
         buffer = ext[number]
@@ -198,11 +218,14 @@
             relay[number - 1].start()
         if number == 1:
             mix()
-            turn()
+            turn_gain()
+            fetch_in.wait()
         if number >= 2:
             to_mate[number - 2].wait()
             relay[number - 2].wait()
             combine(number - 2)
+            for part in range((number - 2) * parts // count, (number - 1) * parts // count):
+                turn(part)
 
     fetch_out.wait()
     tile = 2 * BLOCK
@@ -259,9 +282,18 @@
     turned = pl.pallas_call(
         functools.partial(exchange_kernel, size, owned, chunk, pieces),
         out_shape=jax.ShapeDtypeStruct((bins, nodes), jnp.float32),
-        in_specs=[vmem] * 5 + [smem] * 3 + [vmem] * 2 + [anywhere] * 2,
+        in_specs=[vmem, anywhere, anywhere, vmem]
+        + [anywhere] * 3
+        + [smem]
+        + [vmem] * 2
+        + [anywhere] * 2,
         out_specs=vmem,
         scratch_shapes=[
+            pltpu.VMEM((1, nodes), jnp.float32),
+            pltpu.VMEM((1, nodes), jnp.float32),
+            pltpu.VMEM((slots, BLOCK, BLOCK), jnp.float32),
+            pltpu.SMEM((1, slots), jnp.int32),
+            pltpu.SMEM((1, slots), jnp.int32),
             pltpu.VMEM((slots * BLOCK, nodes), jnp.bfloat16),
             pltpu.VMEM((chunk, slots * BLOCK), jnp.bfloat16),
             pltpu.VMEM((size, count * owned, PIECE), jnp.bfloat16),
@@ -278,11 +310,11 @@
             pltpu.SemaphoreType.DMA((4,)),
             pltpu.SemaphoreType.DMA((size,)),
             pltpu.SemaphoreType.DMA((size,)),
-            pltpu.SemaphoreType.DMA((3,)),
+            pltpu.SemaphoreType.DMA((8,)),
         ]
         + [pltpu.VMEM((5 * owned, chunk, BLOCK), jnp.bfloat16)] * chunks,
         compiler_params=pltpu.CompilerParams(
-            collective_id=0, has_side_effects=True, vmem_limit_bytes=48 * 2**20
+            collective_id=0, has_side_effects=True, vmem_limit_bytes=60 * 2**20
         ),
         name="exchange",
     )(

time: 68.6 us -> 69.1 us (level)
  Pallas kernels: 59.9 us -> 60.7 us
    unnamed x14 -> x4, local copies, waits for them, and re-layouts: 6.33 us -> 4.33 us
    pallas_call x1, Pallas kernels: 59.9 us -> 60.7 us  [shards(): pl.pallas_call(functools.partial(exchange_kernel, size, owned, chunk, pie...]
where the time goes in v4:
time: 69.1 us; the launch traced here: 68.8 us
  Pallas kernels  60.7 us (88%)
  local copies, waits for them, and re-layouts  7.4 us (11%)
  between operations  0.7 us (1%)
    pallas_call x1, Pallas kernels, shards(): pl.pallas_call(functools.partial(exchange_kernel, size, owned, chunk, pie...  60.7 us
    unnamed x4, local copies, waits for them, and re-layouts  4.33 us

profile of v4, /device:TPU:0, one launch (start us, length us, event | category | flops | bytes accessed | tf_op | source)
XLA Modules:
  0.0 68.8 jit_solution(7731517028169389434)
XLA Ops:
  0.0 0.0 copy-start
  0.7 0.1 copy-done
  0.7 0.8 %copy.14 = s32[1,4,2]{2,1,0:T(4,128)S(1)} copy(s32[1,4,2]{1,2,0:T(2,128)} %param.20) | data formatting | bytes 64 | tf_op args[8]
  1.5 0.1 reshape.28
  1.6 0.6 pad.13.list_ref
  2.2 0.7 %pad.14 = f32[1408]{0:T(1024)S(1)} pad(f32[1296]{0:T(1024)} %param.21, f32[]{:T(128)} %constant.13.clone.1), padding=0_112 | pad | bytes 10820 | tf_op jit(solution)/shard_map/jit(_pad)/pad | solution.py:277
  2.9 0.6 reshape.29.gain_row
  3.5 0.1 mul.28
  3.6 0.1 mul.30
  3.7 0.1 mul.32
  3.8 0.1 mul.33
  4.0 0.6 pad.12.mixing
  4.6 60.7 %exchange.1 = f32[1296,512]{1,0:T(8,128)} custom-call(f32[1296,512]{1,0:T(8,128)} %bitcast.7, f32[1,512]{1,0:T(1,128)} %bitcast.10, f32[1,512]{1,0:T(1,128)} %bitcast.11, bf16[4,16,256]{2,1,0:T(8,128)(2,1)} %pad.12.mixing, f32[20,128,128]{2,1,0:T(8,128)} %bitcast.9, s32[1,20]{1,0:T(1,128)} %edge_dst_hbm.1, s32[1,20]{1,0:T(1,128)} %edge_src_hbm.1, ...), custom_call_target="tpu_custom_call" | custom-call | tf_op jit(solution)/shard_map/exchange/pallas_call | solution.py:282
  65.3 3.5 %copy.17 = f32[512,1296]{0,1:T(8,128)} copy(f32[512,1296]{0,1:T(8,128)} %bitcast.6) | data formatting | bytes 5308416
  (4 shorter events, 0.0 us)
Async XLA Ops:
  0.0 0.7 %copy-start = (bf16[64,64]{1,0:T(8,128)(2,1)S(1)}, bf16[64,64]{1,0:T(8,128)(2,1)}, u32[]{:S(2)}) copy-start(bf16[64,64]{1,0:T(8,128)(2,1)} %param.15) | copy-start | bytes 24580

commit v5 on v4

--- a/solution.py
+++ b/solution.py
@@ -314,7 +314,7 @@
         ]
         + [pltpu.VMEM((5 * owned, chunk, BLOCK), jnp.bfloat16)] * chunks,
         compiler_params=pltpu.CompilerParams(
-            collective_id=0, has_side_effects=True, vmem_limit_bytes=60 * 2**20
+            collective_id=0, has_side_effects=True, vmem_limit_bytes=48 * 2**20
         ),
         name="exchange",
     )(

time: 69.1 us -> 67.9 us (0.983)
  Pallas kernels: 60.7 us -> 59.2 us
    unnamed x4 -> x14, local copies, waits for them, and re-layouts: 4.33 us -> 6.33 us
    pallas_call x1, Pallas kernels: 60.7 us -> 59.2 us  [shards(): pl.pallas_call(functools.partial(exchange_kernel, size, owned, chunk, pie...]
where the time goes in v5:
time: 67.9 us; the launch traced here: 67.5 us
  Pallas kernels  59.2 us (87%)
  local copies, waits for them, and re-layouts  7.61 us (11%)
  between operations  0.72 us (1%)
    pallas_call x1, Pallas kernels, shards(): pl.pallas_call(functools.partial(exchange_kernel, size, owned, chunk, pie...  59.2 us
    unnamed x14, local copies, waits for them, and re-layouts  6.33 us

profile of v5, /device:TPU:0, one launch (start us, length us, event | category | flops | bytes accessed | tf_op | source)
XLA Modules:
  0.0 67.5 jit_solution(12052126554632084009)
XLA Ops:
  0.0 0.0 copy-start
  0.7 0.1 copy-done
  0.7 0.8 %copy.14 = s32[1,4,2]{2,1,0:T(4,128)S(1)} copy(s32[1,4,2]{1,2,0:T(2,128)} %param.20) | data formatting | bytes 64 | tf_op args[8]
  1.5 0.1 reshape.28
  1.6 0.7 %pad.14 = f32[1408]{0:T(1024)S(1)} pad(f32[1296]{0:T(1024)} %param.21, f32[]{:T(128)} %constant.13.clone.1), padding=0_112 | pad | bytes 10820 | tf_op jit(solution)/shard_map/jit(_pad)/pad | solution.py:277
  2.3 0.1 mul.28
  2.4 0.1 mul.30
  2.6 0.1 mul.32
  2.7 0.1 mul.33
  2.8 0.0 copy-start.1
  2.8 1.3 %copy-done.1 = f32[1,20,128,128]{3,2,1,0:T(8,128)S(1)} copy-done((f32[1,20,128,128]{3,2,1,0:T(8,128)S(1)}, f32[1,20,128,128]{3,2,1,0:T(8,128)}, u32[]{:S(2)}) %copy-start.1) | copy-done | bytes 1310744
  4.2 0.0 copy-start.2
  4.2 0.7 %copy-done.2 = f32[512]{0:T(512)S(1)} copy-done((f32[512]{0:T(512)S(1)}, f32[512]{0:T(512)}, u32[]{:S(2)}) %copy-start.2) | copy-done | bytes 2072
  4.8 0.0 copy-start.3
  4.8 0.7 %copy-done.3 = f32[512]{0:T(512)S(1)} copy-done((f32[512]{0:T(512)S(1)}, f32[512]{0:T(512)}, u32[]{:S(2)}) %copy-start.3) | copy-done | bytes 2072
  5.5 0.0 copy-start.4
  5.5 0.7 copy-done.4
  6.2 0.0 copy-start.5
  6.2 0.7 copy-done.5
  6.8 59.2 %exchange.1 = f32[1296,512]{1,0:T(8,128)S(1)} custom-call(f32[1296,512]{1,0:T(8,128)} %bitcast.10, f32[1,512]{1,0:T(1,128)S(1)} %bitcast.8, f32[1,512]{1,0:T(1,128)S(1)} %bitcast.9, bf16[4,16,256]{2,1,0:T(8,128)(2,1)S(1)} %pad.12.mixing, f32[20,128,128]{2,1,0:T(8,128)S(1)} %bitcast.7, s32[1,20]{1,0:T(1,128)S(1)} %copy-done.4, s32[1,20]{1,0:T(1,128)S(1)} %copy-done.5, ...), custom_call_target="tpu_custom_call" | custom-call | tf_op jit(solution)/shard_map/exchange/pallas_call | solution.py:282
  66.0 1.5 %copy.17 = f32[512,1296]{0,1:T(8,128)} copy(f32[512,1296]{0,1:T(8,128)S(1)} %bitcast.6) | data formatting | bytes 5308416
  (7 shorter events, 0.1 us)
Async XLA Ops:
  0.0 0.7 %copy-start = (bf16[64,64]{1,0:T(8,128)(2,1)S(1)}, bf16[64,64]{1,0:T(8,128)(2,1)}, u32[]{:S(2)}) copy-start(bf16[64,64]{1,0:T(8,128)(2,1)} %param.15) | copy-start | bytes 24580
  2.8 1.3 %copy-start.1 = (f32[1,20,128,128]{3,2,1,0:T(8,128)S(1)}, f32[1,20,128,128]{3,2,1,0:T(8,128)}, u32[]{:S(2)}) copy-start(f32[1,20,128,128]{3,2,1,0:T(8,128)} %param.16) | copy-start | bytes 3932164
  4.2 0.7 %copy-start.2 = (f32[512]{0:T(512)S(1)}, f32[512]{0:T(512)}, u32[]{:S(2)}) copy-start(f32[512]{0:T(512)} %param.13) | copy-start | bytes 6148
  4.8 0.7 %copy-start.3 = (f32[512]{0:T(512)S(1)}, f32[512]{0:T(512)}, u32[]{:S(2)}) copy-start(f32[512]{0:T(512)} %param.14) | copy-start | bytes 6148
  5.5 0.7 copy-start.4
  6.2 0.7 copy-start.5
